TPU v7x, 256 devices: a whole 4x4x8 slice. The times are simulated.
256 devices in a mesh: loop: 64 (over y_hi, x, z), rep: 4 (over y_lo, core).
Axes of the slice: x: 4, y: 4 (y_hi: 2, y_lo: 2; y = y_hi * 2 + y_lo), z: 8, core: 2. Of those that a mesh axis runs over, the one named last changes fastest.
Arguments:
- teacher_acts: bfloat16 [32768, 16384], P('loop', 'rep'), may hold values from -6 to 6
- gate_weight: bfloat16 [16384, 8192], P('rep', 'loop'), may hold values from -0.046875 to 0.046875
- up_weight: bfloat16 [16384, 8192], P('rep', 'loop'), may hold values from -0.046875 to 0.046875
- down_weight: bfloat16 [8192, 16384], P('loop', 'rep'), may hold values from -0.25 to 0.25
Outputs:
- teacher_out: bfloat16 [32768, 16384], P('loop', 'rep')
All inputs are finite; a program needn't handle non-finite values.
Results may differ from a plain program's by a relative error of at most 0.0049.
Values may be sent and summed in bfloat16 or wider, within the bound.
A program may use at most 128 MiB of HBM per device.

v0:
```python
import jax
import jax.numpy as jnp
from jax import lax
from jax.sharding import PartitionSpec as P

STEPS = 4


def passed_along(block, axis, distance):
    devices = range(lax.axis_size(axis))
    route = [((i - distance) % len(devices), i) for i in devices]
    return lax.ppermute(block, axis, route)


def group_term(acts, packed, width):
    gate_part = packed[:, :width]
    up_part = packed[:, width : 2 * width]
    down_cols = packed[:, 2 * width :]
    partials = (
        jnp.dot(acts, gate_part, preferred_element_type=jnp.float32),
        jnp.dot(acts, up_part, preferred_element_type=jnp.float32),
    )
    gate, upval = lax.psum((partials[0], partials[1]), "rep")
    hidden = (jax.nn.silu(gate) * upval).astype(jnp.bfloat16)
    return lax.dot_general(
        hidden, down_cols, (((1,), (1,)), ((), ())), preferred_element_type=jnp.float32
    )


def body(teacher_acts, gate_weight, up_weight, down_weight):
    width = gate_weight.shape[1]
    packed = jnp.concatenate((gate_weight, up_weight, down_weight.T), axis=1)
    total = group_term(teacher_acts, packed, width)
    held = packed
    for step in range(1, STEPS):
        held = passed_along(held, "loop", 1)
        total = total + group_term(teacher_acts, held, width)
    return total.astype(jnp.bfloat16)


def solution(mesh):
    placed = (P("loop", "rep"), P("rep", "loop"), P("rep", "loop"), P("loop", "rep"))
    return jax.shard_map(
        body, mesh=mesh, in_specs=placed, out_specs=P("loop", "rep"), check_vma=False
    )
```

profile of v0, /device:TPU:1, one launch (start us, length us, event | category | flops | bytes accessed | tf_op | source)
XLA Modules:
  0.0 331.6 jit_solution(9543326281130074023)
XLA Ops:
  6.5 0.0 all-reduce.3.cloned.1.call-start
  6.5 1.6 copy.5
  8.1 0.0 copy-start.2
  8.1 2.4 copy.6
  10.5 0.0 copy-done.1
  10.5 1.5 pad_maximum_fusion
  12.0 0.0 copy-start.3
  12.0 2.5 collective-permute-start
  14.5 76.6 %collective-permute-done = bf16[4096,384]{0,1:T(8,128)(2,1)S(1)} collective-permute-done((bf16[4096,384]{0,1:T(8,128)(2,1)S(1)}, bf16[4096,384]{0,1:T(8,128)(2,1)S(1)}, u32[]{:S(2)}, u32[]{:S(2)}) %collective-permute-start) | collective-permute-done | bytes 3145760 | tf_op jit(solution)/shard_map/ppermute | solution.py:12
  91.1 0.0 collective-permute-start.1
  91.1 74.1 %collective-permute-done.1 = bf16[4096,384]{0,1:T(8,128)(2,1)S(1)} collective-permute-done((bf16[4096,384]{0,1:T(8,128)(2,1)S(1)}, bf16[4096,384]{0,1:T(8,128)(2,1)S(1)}, u32[]{:S(2)}, u32[]{:S(2)}) %collective-permute-start.1) | collective-permute-done | bytes 3145760 | tf_op jit(solution)/shard_map/ppermute | solution.py:12
  165.2 0.0 collective-permute-start.2
  165.2 0.0 copy-done.2
  165.2 0.0 copy-done
  165.2 2.0 fusion.20
  167.2 0.0 copy-done.3
  167.2 2.0 fusion.21
  169.2 2.0 convolution_bitcast_fusion.4
  171.2 1.9 convolution_bitcast_fusion.5
  173.1 2.0 convolution_bitcast_fusion.2
  175.1 2.0 convolution_bitcast_fusion.3
  177.0 61.4 %collective-permute-done.2 = bf16[4096,384]{0,1:T(8,128)(2,1)S(1)} collective-permute-done((bf16[4096,384]{0,1:T(8,128)(2,1)S(1)}, bf16[4096,384]{0,1:T(8,128)(2,1)S(1)}, u32[]{:S(2)}, u32[]{:S(2)}) %collective-permute-start.2) | collective-permute-done | bytes 3145760 | tf_op jit(solution)/shard_map/ppermute | solution.py:12
  238.4 2.0 convolution_bitcast_fusion
  240.4 0.0 copy-done.6
  240.4 2.0 convolution_bitcast_fusion.1
  242.3 0.0 all-reduce.3.cloned.1.call-update
  242.3 58.5 %all-reduce.3.cloned.1.call-done = (f32[512,128]{1,0:T(8,128)}, f32[512,128]{1,0:T(8,128)}, f32[512,128]{1,0:T(8,128)}, f32[512,128]{1,0:T(8,128)}, f32[512,128]...) async-done(((f32[512,128]{1,0:T(8,128)}, f32[512,128]{1,0:T(8,128)}, f32[512,128]{1,0:T(8,128)}, f32[512,128]{1,0:T(8,128)}, ...) | async-done | bytes 2097168 | tf_op jit(solution)/shard_map/psum | solution.py:23
  300.9 5.6 %fusion.11 = f32[512,4096]{1,0:T(8,128)} fusion(bf16[128,4096]{1,0:T(8,128)(2,1)S(1)} %copy-done.1, f32[512,128]{1,0:T(8,128)} %get-tuple-element.7, f32[512,128]{1,0:T(8,128)} %get-tuple-element.8), kind=kOutput, calls=%fused_computation.23 | convolution fusion | flops 537264128 | bytes 9961472 | tf_op jit(solution)/shard_map/dot_general | solution.py:25
  306.5 2.5 fusion.3
  309.1 5.8 %fusion.7 = f32[512,4096]{1,0:T(8,128)} fusion(bf16[4096,384]{0,1:T(8,128)(2,1)} %copy-done.4, f32[512,128]{1,0:T(8,128)S(1)} %copy-done.7, f32[512,128]{1,0:T(8,128)S(1)} %copy-done.8), kind=kOutput, calls=%fused_computation.15 | convolution fusion | flops 537264128 | bytes 9961472 | tf_op jit(solution)/shard_map/dot_general | solution.py:25
  314.9 0.0 copy-done.12
  314.9 9.8 %add_convert_fusion = bf16[512,4096]{1,0:T(8,128)(2,1)} fusion(f32[512,4096]{1,0:T(8,128)S(1)} %fusion.3, f32[512,4096]{1,0:T(8,128)} %fusion.11, f32[512,4096]{1,0:T(8,128)} %fusion.7, bf16[4096,384]{0,1:T(8,128)(2,1)} %copy-done.6, f32[512,128]{1,0:T(8,128)S(1)} %copy-done.11, f32[512,128]{1,0:T(8,128)S(1)} %copy-done.12), kind=kOutput, calls=%fused_computation | convolution fusion | flops 545652736 | bytes 30932992 | tf_op jit(solution)/shard_map/dot_general | solution.py:25
  (18 shorter events, 0.0 us)
Async XLA Ops:
  6.5 4.0 %copy-start.1 = (bf16[128,4096]{1,0:T(8,128)(2,1)S(1)}, bf16[128,4096]{1,0:T(8,128)(2,1)}, u32[]{:S(2)}) copy-start(bf16[128,4096]{1,0:T(8,128)(2,1)} %param.7) | copy-start | bytes 3145732
  6.5 294.3 %all-reduce.3.cloned.1.call-start = ((), (), s32[]{:S(2)}) async-start(), calls=%async_computation | async-start | bytes 4194304 | tf_op jit(solution)/shard_map/psum | solution.py:23
  8.1 157.1 %copy-start.2 = (bf16[4096,128]{1,0:T(8,128)(2,1)S(1)}, bf16[4096,128]{1,0:T(8,128)(2,1)}, u32[]{:S(2)}) copy-start(bf16[4096,128]{1,0:T(8,128)(2,1)} %param.5) | copy-start | bytes 3145732
  10.5 154.8 %copy-start = (bf16[512,4096]{1,0:T(8,128)(2,1)S(1)}, bf16[512,4096]{1,0:T(8,128)(2,1)}, u32[]{:S(2)}) copy-start(bf16[512,4096]{1,0:T(8,128)(2,1)} %param.4) | copy-start | bytes 12582916
  12.0 155.2 %copy-start.3 = (bf16[4096,128]{1,0:T(8,128)(2,1)S(1)}, bf16[4096,128]{1,0:T(8,128)(2,1)}, u32[]{:S(2)}) copy-start(bf16[4096,128]{1,0:T(8,128)(2,1)} %param.6) | copy-start | bytes 3145732
  12.0 79.1 %collective-permute-start = (bf16[4096,384]{0,1:T(8,128)(2,1)S(1)}, bf16[4096,384]{0,1:T(8,128)(2,1)S(1)}, u32[]{:S(2)}, u32[]{:S(2)}) collective-permute-start(bf16[4096,384]{0,1:T(8,128)(2,1)S(1)} %pad_maximum_fusion), channel_id=1, source_target_pairs={{252,0},{0,4},{4,8},{8,12},{12,16},{16,20},{20,24},{24,28},{28,32}... | collective-permute-start | bytes 9437192 | tf_op jit(solution)/shard_map/ppermute | solution.py:12
  91.1 80.0 %copy-start.4 = (bf16[4096,384]{0,1:T(8,128)(2,1)}, bf16[4096,384]{0,1:T(8,128)(2,1)S(1)}, u32[]{:S(2)}) copy-start(bf16[4096,384]{0,1:T(8,128)(2,1)S(1)} %collective-permute-done) | copy-start | bytes 9437188
  91.1 74.1 %collective-permute-start.1 = (bf16[4096,384]{0,1:T(8,128)(2,1)S(1)}, bf16[4096,384]{0,1:T(8,128)(2,1)S(1)}, u32[]{:S(2)}, u32[]{:S(2)}) collective-permute-start(bf16[4096,384]{0,1:T(8,128)(2,1)S(1)} %collective-permute-done), channel_id=1, source_target_pairs={{252,0},{0,4},{4,8},{8,12},{12,16},{16,20},{20,24},{24,28},{28,32}... | collective-permute-start | bytes 9437192 | tf_op jit(solution)/shard_map/ppermute | solution.py:12
  165.2 9.8 %copy-start.5 = (bf16[4096,384]{0,1:T(8,128)(2,1)}, bf16[4096,384]{0,1:T(8,128)(2,1)S(1)}, u32[]{:S(2)}) copy-start(bf16[4096,384]{0,1:T(8,128)(2,1)S(1)} %collective-permute-done.1) | copy-start | bytes 9437188
  165.2 73.2 %collective-permute-start.2 = (bf16[4096,384]{0,1:T(8,128)(2,1)S(1)}, bf16[4096,384]{0,1:T(8,128)(2,1)S(1)}, u32[]{:S(2)}, u32[]{:S(2)}) collective-permute-start(bf16[4096,384]{0,1:T(8,128)(2,1)S(1)} %collective-permute-done.1), channel_id=1, source_target_pairs={{252,0},{0,4},{4,8},{8,12},{12,16},{16,20},{20,24},{24,28},{28,32}... | collective-permute-start | bytes 9437192 | tf_op jit(solution)/shard_map/ppermute | solution.py:12
  238.4 2.0 copy-start.6
  300.9 5.6 %copy-start.9 = (f32[512,128]{1,0:T(8,128)S(1)}, f32[512,128]{1,0:T(8,128)}, u32[]{:S(2)}) copy-start(f32[512,128]{1,0:T(8,128)} %get-tuple-element.5) | copy-start | bytes 786436
  300.9 5.6 %copy-start.10 = (f32[512,128]{1,0:T(8,128)S(1)}, f32[512,128]{1,0:T(8,128)}, u32[]{:S(2)}) copy-start(f32[512,128]{1,0:T(8,128)} %get-tuple-element.6) | copy-start | bytes 786436
  306.5 2.6 copy-start.7
  306.5 2.6 copy-start.8
  309.0 5.8 %copy-start.11 = (f32[512,128]{1,0:T(8,128)S(1)}, f32[512,128]{1,0:T(8,128)}, u32[]{:S(2)}) copy-start(f32[512,128]{1,0:T(8,128)} %get-tuple-element.11) | copy-start | bytes 786436
  309.1 5.8 %copy-start.12 = (f32[512,128]{1,0:T(8,128)S(1)}, f32[512,128]{1,0:T(8,128)}, u32[]{:S(2)}) copy-start(f32[512,128]{1,0:T(8,128)} %get-tuple-element.12) | copy-start | bytes 786436
Sparse Core Ops, SparseCore 0:
  242.5 58.3 all-reduce.2
where the time goes:
time: 332 us
  waiting for transfers between devices  271 us (82%)
  matrix products  39.5 us (12%)
  between operations  13.5 us (4%)
  local copies, waits for them, and re-layouts  3.98 us (1%)
    ppermute x3, waiting for transfers between devices, passed_along(): return lax.ppermute(block, axis, route)  212 us
    psum x1, waiting for transfers between devices, group_term(): gate, upval = lax.psum((partials[0], partials[1]), 'rep')  58.5 us
    dot_general x4, matrix products, group_term(): lax.dot_general(hidden, down_cols, (((1,), (1,)), ((), ())), preferred_el...  23.8 us
    dot_general x4, matrix products, group_term(): jnp.dot(acts, gate_part, preferred_element_type=jnp.float32)  7.87 us
    dot_general x4, matrix products, group_term(): jnp.dot(acts, up_part, preferred_element_type=jnp.float32)  7.84 us
  transfers between devices with their start and end apart: 4, of which 4 were waited for; matrix products, arithmetic and copies ran while one was open for 4% of the time, Pallas kernels for 0%

commit v1 on v0

v1 whole, which is shorter than its diff:
```python
import functools

import jax
import jax.numpy as jnp
from jax import lax
from jax.experimental import pallas as pl
from jax.experimental.pallas import tpu as pltpu
from jax.sharding import PartitionSpec as P

MESH = pl.DeviceIdType.MESH
NQ = 4
NB = 4
ND = 4
NE = 8
F32 = jnp.float32
BF16 = jnp.bfloat16


def dot(a, b):
    return jnp.dot(a, b, preferred_element_type=F32)


def silu_times(gate, up):
    return gate / (1.0 + jnp.exp(-gate)) * up


def kernel(
    n,
    near,
    acts,
    gate,
    up,
    down,
    out,
    a_own,
    a_1,
    a_2,
    w_own,
    w_1,
    w_2,
    dn,
    hid,
    part,
    part_in,
    far_part,
    far_in,
    acc,
    stage,
    stage_in,
    carry,
    carry_in,
    fwd,
    o_buf,
    send_sem,
    recv_sem,
    local_sem,
):
    l, r = lax.axis_index("loop"), lax.axis_index("rep")
    ahead = (lax.rem(l + 1, n), r)
    behind = (lax.rem(l + n - 1, n), r)
    mates = [(l, lax.rem(r + o, NQ)) for o in range(1, NQ)]
    rows, feats = acts.shape
    width = gate.shape[1]
    far = feats - near
    rb = rows // NB
    rq = rb // NQ
    qr = rows // NQ
    started = []

    def remote(src, dst, to):
        i = len(started)
        c = pltpu.make_async_remote_copy(
            src_ref=src,
            dst_ref=dst,
            send_sem=send_sem.at[i],
            recv_sem=recv_sem.at[i],
            device_id=to,
            device_id_type=MESH,
        )
        c.start()
        started.append(c)
        return c

    loads = [
        pltpu.make_async_copy(acts, a_own, local_sem.at[0]),
        pltpu.make_async_copy(gate, w_own.at[0], local_sem.at[1]),
        pltpu.make_async_copy(up, w_own.at[1], local_sem.at[2]),
        pltpu.make_async_copy(down, dn.at[pl.ds(0, width)], local_sem.at[3]),
    ]
    for c in loads:
        c.start()

    barrier = pltpu.get_barrier_semaphore()
    peers = [ahead, behind] + mates
    for p in peers:
        pl.semaphore_signal(barrier, inc=1, device_id=p, device_id_type=MESH)
    pl.semaphore_wait(barrier, len(peers))

    nears, fars = pl.ds(0, near), pl.ds(near, far)

    w1_far = [
        remote(src.at[fars], w_1.at[h, fars], ahead) for h, src in enumerate((gate, up))
    ]
    a1_near = [
        remote(acts.at[pl.ds(i * rb, rb), nears], a_1.at[pl.ds(i * rb, rb), nears], behind)
        for i in range(NB)
    ]
    w1_near = [
        remote(src.at[nears], w_1.at[h, nears], ahead) for h, src in enumerate((gate, up))
    ]

    def weights(ref, at, kc):
        at = pl.multiple_of(at, 128)
        return [ref[0, pl.ds(at, kc), :], ref[1, pl.ds(at, kc), :]]

    def whole(a_ref, w_ref, count, acc_ref):
        kc = 256
        acc_ref[...] = jnp.zeros_like(acc_ref)

        def step(k, _):
            at = pl.multiple_of(k * kc, kc)
            w = jnp.concatenate(weights(w_ref, at, kc), axis=1)
            acc_ref[...] += dot(a_ref[:, pl.ds(at, kc)], w)
            return 0

        lax.fori_loop(0, count // kc, step, 0)

    def scatter(buf, into):
        return [remote(buf.at[to[1]], into.at[o], to) for o, to in enumerate(mates)]

    def own_pair(s, w_ref):
        whole(a_own, w_ref, feats, acc)
        for q in range(NQ):
            part[s, q] = acc[q * qr : (q + 1) * qr, :]
        return scatter(part.at[s], part_in.at[s])

    def own_hidden(s, copies):
        for c in copies:
            c.wait_recv()
        total = part[s, r] + part_in[s, 0] + part_in[s, 1] + part_in[s, 2]
        value = silu_times(total[:, :width], total[:, width:])
        at = (pl.ds(pl.multiple_of(r * qr, qr), qr), pl.ds(s * width, width))
        hid[at] = value.astype(BF16)
        return [remote(hid.at[at], hid.at[at], to) for to in mates]

    gathers = []
    for c in loads:
        c.wait()
    copies = own_pair(0, w_own)
    gathers += own_hidden(0, copies)

    a2 = []

    def relay_a(i):
        a1_near[i].wait_recv()
        at = (pl.ds(i * rb, rb), nears)
        a2.append(remote(a_1.at[at], a_2.at[pl.ds(i * rb, rb)], behind))

    relay_a(0)
    relay_a(1)
    relay_a(2)
    w2_far = []
    for h in range(2):
        w1_far[h].wait_recv()
        w2_far.append(remote(w_1.at[h, fars], w_2.at[h], ahead))
    relay_a(3)
    a1_far = [
        remote(acts.at[pl.ds(i * rb, rb), fars], a_1.at[pl.ds(i * rb, rb), fars], behind)
        for i in range(NB)
    ]
    for c in w1_near:
        c.wait_recv()
    copies = own_pair(1, w_1)
    gathers += own_hidden(1, copies)
    whole(a_1, w_1, near, acc)

    d1 = []
    for i in range(NB):
        if i == NB - 1:
            for j in range(ND):
                at = pl.ds(j * (feats // ND), feats // ND)
                d1.append(remote(down.at[:, at], dn.at[pl.ds(width, width), at], ahead))
        a2[i].wait_recv()
        kc = 256

        def near_step(k, total, i=i):
            at = pl.multiple_of(k * kc, kc)
            w = jnp.concatenate(weights(w_1, at, kc), axis=1)
            return total + dot(a_2[pl.ds(i * rb, rb), pl.ds(at, kc)], w)

        total = lax.fori_loop(0, near // kc, near_step, jnp.zeros((rb, 2 * width), F32))
        for q in range(NQ):
            far_part[q, i] = total[q * rq : (q + 1) * rq, :]
    copies = scatter(far_part, far_in)
    for c in copies:
        c.wait_recv()
    carry[...] = far_part[r] + far_in[0] + far_in[1] + far_in[2]
    carried = remote(carry, carry_in, ahead)

    for c in w2_far:
        c.wait_recv()

    d2, d3 = [], []

    def relay_d2(j):
        d1[j].wait_recv()
        at = pl.ds(j * (feats // ND), feats // ND)
        d2.append(
            remote(dn.at[pl.ds(width, width), at], dn.at[pl.ds(2 * width, width), at], ahead)
        )

    def relay_d3(j):
        d2[j].wait_recv()
        for e in range(j * NE // ND, (j + 1) * NE // ND):
            at = pl.ds(e * (feats // NE), feats // NE)
            d3.append(
                remote(
                    dn.at[pl.ds(2 * width, width), at],
                    dn.at[pl.ds(3 * width, width), at],
                    ahead,
                )
            )

    later = pl.ds(2 * width, 2 * width)

    def stage_rows(i):
        a1_far[i].wait_recv()
        kc = 256

        def far_step(k, total):
            at = pl.multiple_of(k * kc, kc)
            there = pl.multiple_of(near + at, kc)
            w = jnp.concatenate(weights(w_1, there, kc) + weights(w_2, at, kc), axis=1)
            return total + dot(a_1[pl.ds(i * rb, rb), pl.ds(there, kc)], w)

        total = lax.fori_loop(0, far // kc, far_step, jnp.zeros((rb, 4 * width), F32))
        for q in range(NQ):
            at = pl.ds(q * rq, rq)
            mine = total[q * rq : (q + 1) * rq, :]
            stage[i, q, :, : 2 * width] = mine[:, : 2 * width] + acc[pl.ds(i * rb + q * rq, rq), :]
            stage[i, q, :, 2 * width :] = mine[:, 2 * width :]
        copies = scatter(stage.at[i], stage_in.at[i])
        if i == 0:
            carried.wait_recv()
        for c in copies:
            c.wait_recv()
        total = stage[i, r] + stage_in[i, 0] + stage_in[i, 1] + stage_in[i, 2]
        one, two = total[:, : 2 * width], total[:, 2 * width :] + carry_in[i]
        fwd[i, :, :width] = silu_times(one[:, :width], one[:, width:]).astype(BF16)
        fwd[i, :, width:] = silu_times(two[:, :width], two[:, width:]).astype(BF16)
        at = (pl.ds(pl.multiple_of(i * rb + r * rq, rq), rq), later)
        sent = remote(fwd.at[i], hid.at[at], ahead)
        sent.wait_recv()
        return [remote(hid.at[at], hid.at[at], to) for to in mates]

    gathers += stage_rows(0)
    relay_d2(0)
    relay_d2(1)
    relay_d2(2)
    gathers += stage_rows(1)
    relay_d2(3)
    relay_d3(0)
    relay_d3(1)
    gathers += stage_rows(2)
    relay_d3(2)
    relay_d3(3)
    gathers += stage_rows(3)
    for c in gathers:
        c.wait_recv()

    stores = []
    for e in range(NE):
        d3[e].wait_recv()
        cols = feats // NE
        at = pl.ds(e * cols, cols)
        o_buf[:, at] = dot(hid[...], dn[:, at]).astype(BF16)
        c = pltpu.make_async_copy(o_buf.at[:, at], out.at[:, at], local_sem.at[4 + e])
        c.start()
        stores.append(c)
    for c in started:
        c.wait_send()
    for c in stores:
        c.wait()


COPIES = 96


def body(n, near, acts, gate, up, down):
    rows, feats = acts.shape
    width = gate.shape[1]
    far = feats - near
    rb, qr = rows // NB, rows // NQ
    rq = rb // NQ
    any_space = pl.BlockSpec(memory_space=pl.ANY)
    vmem = pltpu.VMEM
    return pl.pallas_call(
        functools.partial(kernel, n, near),
        out_shape=jax.ShapeDtypeStruct((rows, feats), BF16),
        in_specs=[any_space] * 4,
        out_specs=any_space,
        scratch_shapes=[
            vmem((rows, feats), BF16),
            vmem((rows, feats), BF16),
            vmem((rows, near), BF16),
            vmem((2, feats, width), BF16),
            vmem((2, feats, width), BF16),
            vmem((2, far, width), BF16),
            vmem((4 * width, feats), BF16),
            vmem((rows, 4 * width), BF16),
            vmem((2, NQ, qr, 2 * width), F32),
            vmem((2, NQ - 1, qr, 2 * width), F32),
            vmem((NQ, NB, rq, 2 * width), F32),
            vmem((NQ - 1, NB, rq, 2 * width), F32),
            vmem((rows, 2 * width), F32),
            vmem((NB, NQ, rq, 4 * width), F32),
            vmem((NB, NQ - 1, rq, 4 * width), F32),
            vmem((NB, rq, 2 * width), F32),
            vmem((NB, rq, 2 * width), F32),
            vmem((NB, rq, 2 * width), BF16),
            vmem((rows, feats), BF16),
            pltpu.SemaphoreType.DMA((COPIES,)),
            pltpu.SemaphoreType.DMA((COPIES,)),
            pltpu.SemaphoreType.DMA((4 + NE,)),
        ],
        compiler_params=pltpu.CompilerParams(
            collective_id=0, has_side_effects=True, vmem_limit_bytes=56 * 2**20
        ),
    )(acts, gate, up, down)


NEAR = 6


def solution(mesh):
    n = mesh.shape["loop"]
    placed = (P("loop", "rep"), P("rep", "loop"), P("rep", "loop"), P("loop", "rep"))

    def step(acts, gate, up, down):
        return body(n, acts.shape[1] // 16 * NEAR, acts, gate, up, down)

    return jax.shard_map(
        step, mesh=mesh, in_specs=placed, out_specs=P("loop", "rep"), check_vma=False
    )
```

time: 332 us -> 292 us (0.88)
  the two profiles are of different devices: /device:TPU:1 before, /device:TPU:105 now
where the time goes in v1:
time: 292 us
  Pallas kernels  287 us (98%)
  local copies, waits for them, and re-layouts  4.7 us (2%)
    pallas_call x1, Pallas kernels, body(): pl.pallas_call(functools.partial(kernel, n, near), out_shape=jax.ShapeDty...  287 us

profile of v1, /device:TPU:105, one launch (start us, length us, event | category | flops | bytes accessed | tf_op | source)
XLA Modules:
  0.0 291.7 jit_solution(11744846381573514968)
XLA Ops:
  0.0 287.0 %shard_map.46 = bf16[512,4096]{1,0:T(8,128)(2,1)} custom-call(bf16[512,4096]{1,0:T(8,128)(2,1)} %acts.1, bf16[4096,128]{1,0:T(8,128)(2,1)} %gate.1, bf16[4096,128]{1,0:T(8,128)(2,1)} %up.1, bf16[128,4096]{1,0:T(8,128)(2,1)} %down.1), custom_call_target="tpu_custom_call" | custom-call | tf_op jit(solution)/shard_map/pallas_call | solution.py:297
  287.0 4.7 %copy.6 = bf16[512,4096]{1,0:T(8,128)(2,1)} copy(bf16[512,4096]{1,0:T(8,128)(2,1)} %shard_map.46) | data formatting | bytes 8388608

commit v2 on v1

v2 whole, which is shorter than its diff:
```python
import functools

import jax
import jax.numpy as jnp
from jax import lax
from jax.experimental import pallas as pl
from jax.experimental.pallas import tpu as pltpu
from jax.sharding import PartitionSpec as P

MESH = pl.DeviceIdType.MESH
NEAR = 5
NB = 4
NA = 16
ND = 8
WINDOW = 3
CROSS = 3
LAG = 5
COPIES = 192
F32 = jnp.float32
BF16 = jnp.bfloat16


def dot(a, b):
    return jnp.dot(a, b, preferred_element_type=F32)


def silu_times(gate, up):
    return gate / (1.0 + jnp.exp(-gate)) * up


def kernel(
    n,
    near,
    acts,
    gate,
    up,
    down,
    out,
    a_own,
    a_1,
    a_2,
    w_own,
    w_1,
    w_2,
    dn,
    hid,
    part,
    part_in,
    half_in,
    far_part,
    far_in,
    far_half,
    acc,
    stage,
    stage_in,
    stage_half,
    carry,
    carry_in,
    fwd,
    o_buf,
    v_w1,
    v_w2,
    v_d,
    v_a1,
    v_a2,
    v_carry,
    v_fwd,
    send_sem,
    recv_sem,
    pass_sem,
    on_sem,
    local_sem,
):
    l, r = lax.axis_index("loop"), lax.axis_index("rep")
    core, y = lax.rem(r, 2), lax.div(r, 2)
    ahead = (lax.rem(l + 1, n), r)
    behind = (lax.rem(l + n - 1, n), r)
    half = n // 2
    first, final = lax.rem(l, half) == 0, lax.rem(l, half) == half - 1
    other = lax.rem(r + 2, 4)
    partner = (lax.rem(l + half, n), other)
    ahead_via = (lax.rem(l + 1 + half, n), other)
    behind_via = (lax.rem(l + n - 1 + half, n), other)
    twin = (l, r + 1 - 2 * core)
    across = (l, lax.rem(r + 2, 4))
    rows, feats = acts.shape
    width = gate.shape[1]
    far = feats - near
    rb = rows // NB
    ra = rows // NA
    rq = rb // 4
    qr = rows // 4
    mine = 2 * core + y
    started = []

    def remote(src, dst, to):
        i = len(started)
        c = pltpu.make_async_remote_copy(
            src_ref=src,
            dst_ref=dst,
            send_sem=send_sem.at[i],
            recv_sem=recv_sem.at[i],
            device_id=to,
            device_id_type=MESH,
        )
        c.start()
        started.append(c)
        return c

    class Hop:
        def __init__(self, src, dst, by, to, on=None):
            self.i = i = len(started)
            self.by, self.on = by, dst if on is None else on
            self.end, self.via = (final, first) if to is ahead else (first, final)
            self.id = id(self)
            whole = pltpu.make_async_remote_copy(
                src_ref=src,
                dst_ref=dst,
                send_sem=send_sem.at[i],
                recv_sem=recv_sem.at[i],
                device_id=to,
                device_id_type=MESH,
            )
            leg = pltpu.make_async_remote_copy(
                src_ref=src,
                dst_ref=by,
                send_sem=send_sem.at[i],
                recv_sem=pass_sem.at[i],
                device_id=ahead_via if to is ahead else behind_via,
                device_id_type=MESH,
            )
            self.whole, self.leg = whole, leg
            pl.when(self.end)(leg.start)
            pl.when(jnp.logical_not(self.end))(whole.start)
            started.append(self)
            hops.append(self)

        def pass_on(self):
            if self in passed:
                return
            passed.append(self)
            second = pltpu.make_async_remote_copy(
                src_ref=self.by,
                dst_ref=self.on,
                send_sem=on_sem.at[self.i],
                recv_sem=recv_sem.at[self.i],
                device_id=partner,
                device_id_type=MESH,
            )
            self.second = second

            @pl.when(self.via)
            def _():
                self.leg.wait_recv()
                second.start()

        def wait_send(self):
            self.whole.wait_send()

        def wait_recv(self):
            self.whole.wait_recv()

    hops, passed = [], []
    here = set()

    def arrive(c):
        if id(c) not in here:
            here.add(id(c))
            c.wait_recv()

    loads = [
        pltpu.make_async_copy(acts, a_own, local_sem.at[0]),
        pltpu.make_async_copy(gate, w_own.at[0], local_sem.at[1]),
        pltpu.make_async_copy(up, w_own.at[1], local_sem.at[2]),
        pltpu.make_async_copy(down, dn.at[pl.ds(0, width)], local_sem.at[3]),
    ]
    for c in loads:
        c.start()

    barrier = pltpu.get_barrier_semaphore()
    def greet(p):
        pl.semaphore_signal(barrier, inc=1, device_id=p, device_id_type=MESH)

    def choose(cond, one, two):
        return tuple(jnp.where(cond, a, b) for a, b in zip(one, two))

    for p in (choose(final, ahead_via, ahead), choose(first, behind_via, behind), twin, across):
        greet(p)

    @pl.when(jnp.logical_or(first, final))
    def _():
        greet(partner)
        pl.semaphore_wait(barrier, 5)

    @pl.when(jnp.logical_not(jnp.logical_or(first, final)))
    def _():
        pl.semaphore_wait(barrier, 4)

    landed = WINDOW + 1
    crossed = landed + CROSS
    unit = feats * width // ND
    kw = unit // (2 * width)
    w1, w2, d1, d2, d3 = {}, {}, {}, {}, {}
    a1n, a2, a1f = {}, {}, {}

    def send_w(at):
        def go():
            ds = pl.ds(at, kw)
            w1[at] = [
                Hop(s.at[ds], w_1.at[h, ds], v_w1.at[h, ds], ahead) for h, s in enumerate((gate, up))
            ]
            return w1[at]

        return kw * 2 * width / unit, go

    def relay_w(at):
        def go():
            for c in w1[at]:
                arrive(c)
            src, dst = pl.ds(at, kw), pl.ds(at - near, kw)
            w2[at] = [
                Hop(w_1.at[h, src], w_2.at[h, dst], v_w2.at[h, dst], ahead) for h in range(2)
            ]
            return w2[at]

        return kw * 2 * width / unit, go

    def send_d(j):
        def go():
            at = pl.ds(j * (feats // ND), feats // ND)
            d1[j] = Hop(down.at[:, at], dn.at[pl.ds(width, width), at], v_d.at[0, :, at], ahead)
            return [d1[j]]

        return 1, go

    def relay_d(hop, j):
        def go():
            source, made = (d1, d2) if hop == 2 else (d2, d3)
            arrive(source[j])
            at = pl.ds(j * (feats // ND), feats // ND)
            made[j] = Hop(
                dn.at[pl.ds((hop - 1) * width, width), at],
                dn.at[pl.ds(hop * width, width), at],
                v_d.at[hop - 1, :, at],
                ahead,
            )
            return [made[j]]

        return 1, go

    def send_a(store, i, at, count):
        def go():
            ds = (pl.ds(i * ra, ra), pl.ds(at, count))
            store[i] = Hop(acts.at[ds], a_1.at[ds], v_a1.at[ds], behind)
            return [store[i]]

        return ra * count / unit, go

    def relay_a(i):
        def go():
            arrive(a1n[i])
            ds = (pl.ds(i * ra, ra), pl.ds(0, near))
            to = pl.ds(i * ra, ra)
            a2[i] = Hop(a_1.at[ds], a_2.at[to], v_a2.at[to], behind)
            return [a2[i]]

        return ra * near / unit, go

    ahead_stream = [send_w(at) for at in range(near, feats, kw)]
    ahead_stream += [send_w(at) for at in range(0, near, kw)]
    ahead_stream += [relay_w(at) for at in range(near, feats, kw)]
    ahead_stream += [send_d(j) for j in range(ND)]
    ahead_stream += [relay_d(2, j) for j in range(ND)]
    ahead_stream += [relay_d(3, j) for j in range(ND)]
    back_stream = [send_a(a1n, i, 0, near) for i in range(NA)]
    back_stream += [relay_a(i) for i in range(NA)]
    back_stream += [send_a(a1f, i, near, far) for i in range(NA)]

    def weights(ref, at, kc):
        return [ref[0, pl.ds(at, kc), :], ref[1, pl.ds(at, kc), :]]

    def whole(a_ref, w_ref, count):
        kc = feats // 16
        acc[...] = jnp.zeros_like(acc)

        def step(k, _):
            at = pl.multiple_of(k * kc, kc)
            w = jnp.concatenate(weights(w_ref, at, kc), axis=1)
            acc[...] += dot(a_ref[:, pl.ds(at, kc)], w)
            return 0

        lax.fori_loop(0, count // kc, step, 0)

    def reduce_1(buf, into):
        return remote(buf.at[1 - core], into, twin)

    def reduce_2(copy, buf, into, half):
        arrive(copy)
        into[...] = into[...] + buf[core]
        return remote(into.at[1 - y], half, across)

    def reduce_3(copy, into, half):
        arrive(copy)
        return into[y] + half[...]

    def gather_1(at):
        return remote(hid.at[at], hid.at[at], twin), remote(hid.at[at], hid.at[at], across)

    def gather_2(copies, at):
        arrive(copies[1])
        return copies[0], remote(hid.at[at], hid.at[at], twin)

    todo = {}

    def when(step):
        def note(f):
            todo.setdefault(step, []).append(f)
            return f

        return note

    arrivals = []
    state = {}

    def own_at(s, block):
        at = pl.multiple_of(block * qr, qr)
        return pl.ds(at, qr), pl.ds(s * width, width)

    def own_pair(s, step, w_ref, ready):
        @when(step)
        def _():
            ready()
            whole(a_own, w_ref, feats)
            for q in range(4):
                part[s, q // 2, q % 2] = acc[q * qr : (q + 1) * qr, :]
            state["p", s] = reduce_1(part.at[s], part_in.at[s])

        @when(step + 1)
        def _():
            state["p", s] = reduce_2(state["p", s], part.at[s], part_in.at[s], half_in.at[s])

        @when(step + 1 + LAG)
        def _():
            total = reduce_3(state["p", s], part_in.at[s], half_in.at[s])
            hid[own_at(s, mine)] = silu_times(total[:, :width], total[:, width:]).astype(BF16)
            state["p", s] = gather_1(own_at(s, mine))

        @when(step + 1 + 2 * LAG)
        def _():
            arrivals.extend(gather_2(state["p", s], own_at(s, 2 * core + 1 - y)))

    def loaded():
        for c in loads:
            c.wait()

    def arrived():
        for cs in w1.values():
            for c in cs:
                arrive(c)

    size_w, size_a = feats * 2 * width / unit, rows * near / unit
    size_f = rows * far / unit
    step_1 = int(size_w) + crossed
    step_c = max(step_1 + 1, int(2 * size_a) + crossed)
    own_pair(0, 0, w_own, loaded)
    own_pair(1, step_1, w_1, arrived)

    @when(step_1)
    def _():
        for i in range(NA):
            arrive(a1n[i])
        whole(a_1, w_1, near)

    @when(step_c)
    def _():
        kc = feats // 16
        for i in range(NA):
            arrive(a2[i])
        for i in range(NB):

            def near_step(k, total, i=i):
                at = pl.multiple_of(k * kc, kc)
                w = jnp.concatenate(weights(w_1, at, kc), axis=1)
                return total + dot(a_2[pl.ds(i * rb, rb), pl.ds(at, kc)], w)

            total = lax.fori_loop(0, near // kc, near_step, jnp.zeros((rb, 2 * width), F32))
            for q in range(4):
                far_part[q // 2, q % 2, i] = total[q * rq : (q + 1) * rq, :]
        state["c"] = reduce_1(far_part, far_in)

    @when(step_c + 1)
    def _():
        state["c"] = reduce_2(state["c"], far_part, far_in, far_half)

    @when(step_c + 1 + LAG)
    def _():
        carry[...] = reduce_3(state["c"], far_in, far_half)
        state["c"] = Hop(carry, carry_in, v_carry, ahead)

    def stage_at(i, block):
        at = pl.multiple_of(i * rb + block * rq, rq)
        return pl.ds(at, rq), pl.ds(2 * width, 2 * width)

    def stage_a(i):
        kc = feats // 16
        for j in range(i * NA // NB, (i + 1) * NA // NB):
            arrive(a1f[j])
        if i == 0:
            for cs in w2.values():
                for c in cs:
                    arrive(c)

        def far_step(k, total):
            at = pl.multiple_of(k * kc, kc)
            there = pl.multiple_of(near + at, kc)
            w = jnp.concatenate(weights(w_1, there, kc) + weights(w_2, at, kc), axis=1)
            return total + dot(a_1[pl.ds(i * rb, rb), pl.ds(there, kc)], w)

        total = lax.fori_loop(0, far // kc, far_step, jnp.zeros((rb, 4 * width), F32))
        for q in range(4):
            this = total[q * rq : (q + 1) * rq, :]
            first = this[:, : 2 * width] + acc[pl.ds(i * rb + q * rq, rq), :]
            stage[i, q // 2, q % 2, :, : 2 * width] = first
            stage[i, q // 2, q % 2, :, 2 * width :] = this[:, 2 * width :]
        state["s", i] = reduce_1(stage.at[i], stage_in.at[i])

    def stage_b(i):
        state["s", i] = reduce_2(state["s", i], stage.at[i], stage_in.at[i], stage_half.at[i])

    def stage_c(i):
        if i == 0:
            state["c"].pass_on()
            arrive(state["c"])
        total = reduce_3(state["s", i], stage_in.at[i], stage_half.at[i])
        one, two = total[:, : 2 * width], total[:, 2 * width :] + carry_in[i]
        fwd[i, :, :width] = silu_times(one[:, :width], one[:, width:]).astype(BF16)
        fwd[i, :, width:] = silu_times(two[:, :width], two[:, width:]).astype(BF16)
        state["s", i] = Hop(
            fwd.at[i],
            hid.at[stage_at(i, mine)],
            v_fwd.at[i],
            ahead,
            hid.at[stage_at(i, 2 * core + 1 - y)],
        )

    def stage_d(i):
        state["s", i].pass_on()
        arrive(state["s", i])
        state["s", i] = gather_1(stage_at(i, mine))

    def stage_e(i):
        arrivals.extend(gather_2(state["s", i], stage_at(i, 2 * core + 1 - y)))

    last = int(2 * size_w - size_w * near / feats + 3 * ND) + 1
    for i in range(NB):
        step = int(2 * size_a + size_f * (i + 1) / NB) + crossed
        later = (0, 1, 1 + LAG, 1 + LAG + crossed, 1 + 2 * LAG + crossed)
        for f, j in zip((stage_a, stage_b, stage_c, stage_d, stage_e), later):
            when(min(step + j, last))(functools.partial(f, i))

    queues = []
    for stream in (ahead_stream, back_stream):
        due, total = [], 0.0
        for size, go in stream:
            due.append((int(total + 1e-6), go))
            total += size
        queues.append([due, 0, []])
    for step in range(last + 1):
        for queue in queues:
            due, place, sent = queue
            for copies in [c for at, c in sent if at == step - landed]:
                for c in copies:
                    c.pass_on()
            for copies in [c for at, c in sent if at == step - WINDOW]:
                for c in copies:
                    c.wait_send()
            while place < len(due) and due[place][0] <= step:
                sent.append((step, due[place][1]()))
                place += 1
            queue[1] = place
        for f in todo.get(step, []):
            f()
            if step == last:
                for c in hops:
                    c.pass_on()
        if step == last:
            for c in hops:
                c.pass_on()
    for due, place, _ in queues:
        assert place == len(due)
    assert len(started) <= COPIES

    for c in arrivals:
        arrive(c)
    stores = []
    for e in range(ND):
        arrive(d3[e])
        cols = feats // ND
        at = pl.ds(e * cols, cols)
        o_buf[:, at] = dot(hid[...], dn[:, at]).astype(BF16)
        c = pltpu.make_async_copy(o_buf.at[:, at], out.at[:, at], local_sem.at[4 + e])
        c.start()
        stores.append(c)
    waited = {id(c) for _, _, sent in queues for at, cs in sent if at + WINDOW <= last for c in cs}
    for c in started:
        if id(c) not in waited:
            c.wait_send()
    for c in hops:
        pl.when(c.via)(c.second.wait_send)
    for c in stores:
        c.wait()


def body(n, near, acts, gate, up, down):
    rows, feats = acts.shape
    width = gate.shape[1]
    far = feats - near
    rb, qr = rows // NB, rows // 4
    rq = rb // 4
    any_space = pl.BlockSpec(memory_space=pl.ANY)
    vmem = pltpu.VMEM
    return pl.pallas_call(
        functools.partial(kernel, n, near),
        out_shape=jax.ShapeDtypeStruct((rows, feats), BF16),
        in_specs=[any_space] * 4,
        out_specs=any_space,
        scratch_shapes=[
            vmem((rows, feats), BF16),
            vmem((rows, feats), BF16),
            vmem((rows, near), BF16),
            vmem((2, feats, width), BF16),
            vmem((2, feats, width), BF16),
            vmem((2, far, width), BF16),
            vmem((4 * width, feats), BF16),
            vmem((rows, 4 * width), BF16),
            vmem((2, 2, 2, qr, 2 * width), F32),
            vmem((2, 2, qr, 2 * width), F32),
            vmem((2, qr, 2 * width), F32),
            vmem((2, 2, NB, rq, 2 * width), F32),
            vmem((2, NB, rq, 2 * width), F32),
            vmem((NB, rq, 2 * width), F32),
            vmem((rows, 2 * width), F32),
            vmem((NB, 2, 2, rq, 4 * width), F32),
            vmem((NB, 2, rq, 4 * width), F32),
            vmem((NB, rq, 4 * width), F32),
            vmem((NB, rq, 2 * width), F32),
            vmem((NB, rq, 2 * width), F32),
            vmem((NB, rq, 2 * width), BF16),
            vmem((rows, feats), BF16),
            vmem((2, feats, width), BF16),
            vmem((2, far, width), BF16),
            vmem((3, width, feats), BF16),
            vmem((rows, feats), BF16),
            vmem((rows, near), BF16),
            vmem((NB, rq, 2 * width), F32),
            vmem((NB, rq, 2 * width), BF16),
            pltpu.SemaphoreType.DMA((COPIES,)),
            pltpu.SemaphoreType.DMA((COPIES,)),
            pltpu.SemaphoreType.DMA((COPIES,)),
            pltpu.SemaphoreType.DMA((COPIES,)),
            pltpu.SemaphoreType.DMA((4 + ND,)),
        ],
        compiler_params=pltpu.CompilerParams(
            collective_id=0, has_side_effects=True, vmem_limit_bytes=56 * 2**20
        ),
    )(acts, gate, up, down)


def solution(mesh):
    n = mesh.shape["loop"]
    placed = (P("loop", "rep"), P("rep", "loop"), P("rep", "loop"), P("loop", "rep"))

    def step(acts, gate, up, down):
        return body(n, acts.shape[1] // 16 * NEAR, acts, gate, up, down)

    return jax.shard_map(
        step, mesh=mesh, in_specs=placed, out_specs=P("loop", "rep"), check_vma=False
    )
```

time: 292 us -> 240 us (0.82)
  the two profiles are of different devices: /device:TPU:105 before, /device:TPU:1 now
where the time goes in v2:
time: 240 us
  Pallas kernels  235 us (98%)
  local copies, waits for them, and re-layouts  4.7 us (2%)
    pallas_call x1, Pallas kernels, body(): pl.pallas_call(functools.partial(kernel, n, near), out_shape=jax.ShapeDty...  235 us

profile of v2, /device:TPU:1, one launch (start us, length us, event | category | flops | bytes accessed | tf_op | source)
XLA Modules:
  0.0 239.6 jit_solution(3394709845470878876)
XLA Ops:
  0.0 234.9 %shard_map.46 = bf16[512,4096]{1,0:T(8,128)(2,1)} custom-call(bf16[512,4096]{1,0:T(8,128)(2,1)} %acts.1, bf16[4096,128]{1,0:T(8,128)(2,1)} %gate.1, bf16[4096,128]{1,0:T(8,128)(2,1)} %up.1, bf16[128,4096]{1,0:T(8,128)(2,1)} %down.1), custom_call_target="tpu_custom_call" | custom-call | tf_op jit(solution)/shard_map/pallas_call | solution.py:522
  234.9 4.7 %copy.6 = bf16[512,4096]{1,0:T(8,128)(2,1)} copy(bf16[512,4096]{1,0:T(8,128)(2,1)} %shard_map.46) | data formatting | bytes 8388608

commit v3 on v2

v3 whole, which is shorter than its diff:
```python
import functools

import jax
import jax.numpy as jnp
from jax import lax
from jax.experimental import pallas as pl
from jax.experimental.pallas import tpu as pltpu
from jax.sharding import PartitionSpec as P

MESH = pl.DeviceIdType.MESH
NA = 16
ND = 8
WINDOW = 3
PASS = 4
CROSS = 3
LAG = 5
COPIES = 136
F32 = jnp.float32
BF16 = jnp.bfloat16


def dot(a, b):
    return jnp.dot(a, b, preferred_element_type=F32)


def silu_times(gate, up):
    return gate / (1.0 + jnp.exp(-gate)) * up


def kernel(
    n,
    acts,
    gate,
    up,
    down,
    out,
    a_own,
    a_1,
    w_own,
    w_1,
    w_2,
    dn,
    hid,
    acc,
    part,
    part_in,
    half_in,
    fwd,
    o_buf,
    v_w1,
    v_w2,
    v_d,
    v_a1,
    v_fwd,
    send_sem,
    recv_sem,
    pass_sem,
    on_sem,
    local_sem,
):
    l, r = lax.axis_index("loop"), lax.axis_index("rep")
    core, y = lax.rem(r, 2), lax.div(r, 2)
    ahead = (lax.rem(l + 1, n), r)
    behind = (lax.rem(l + n - 1, n), r)
    half = n // 2
    first, final = lax.rem(l, half) == 0, lax.rem(l, half) == half - 1
    other = lax.rem(r + 2, 4)
    partner = (lax.rem(l + half, n), other)
    ahead_via = (lax.rem(l + 1 + half, n), other)
    behind_via = (lax.rem(l + n - 1 + half, n), other)
    ahead_other = (lax.rem(l + 1, n), other)
    behind_other = (lax.rem(l + n - 1, n), other)
    twin = (l, r + 1 - 2 * core)
    across = (l, lax.rem(r + 2, 4))
    rows, feats = acts.shape
    width = gate.shape[1]
    ra = rows // NA
    qr = rows // 4
    mine = 2 * core + y
    started = []

    def remote(src, dst, to):
        i = len(started)
        c = pltpu.make_async_remote_copy(
            src_ref=src,
            dst_ref=dst,
            send_sem=send_sem.at[i],
            recv_sem=recv_sem.at[i],
            device_id=to,
            device_id_type=MESH,
        )
        c.start()
        started.append(c)
        return c

    class Hop:
        def __init__(self, src, dst, by, to, on=None, mate=False):
            self.i = i = len(started)
            self.by, self.on = by, dst if on is None else on
            self.end, self.via = (final, first) if to is ahead else (first, final)
            self.partner = partner
            handed = ahead_via if to is ahead else behind_via
            if mate:
                self.via, handed, self.partner = final, across, ahead_other
            whole = pltpu.make_async_remote_copy(
                src_ref=src,
                dst_ref=dst,
                send_sem=send_sem.at[i],
                recv_sem=recv_sem.at[i],
                device_id=to,
                device_id_type=MESH,
            )
            leg = pltpu.make_async_remote_copy(
                src_ref=src,
                dst_ref=by,
                send_sem=send_sem.at[i],
                recv_sem=pass_sem.at[i],
                device_id=handed,
                device_id_type=MESH,
            )
            self.whole, self.leg = whole, leg
            pl.when(self.end)(leg.start)
            pl.when(jnp.logical_not(self.end))(whole.start)
            started.append(self)
            hops.append(self)

        def pass_on(self):
            if self in passed:
                return
            passed.append(self)
            second = pltpu.make_async_remote_copy(
                src_ref=self.by,
                dst_ref=self.on,
                send_sem=on_sem.at[self.i],
                recv_sem=recv_sem.at[self.i],
                device_id=self.partner,
                device_id_type=MESH,
            )
            self.second = second

            @pl.when(self.via)
            def _():
                self.leg.wait_recv()
                second.start()

        def wait_send(self):
            self.whole.wait_send()

        def wait_recv(self):
            self.whole.wait_recv()

    hops, passed = [], []
    here = set()

    def arrive(c):
        if id(c) not in here:
            here.add(id(c))
            c.wait_recv()

    loads = [
        pltpu.make_async_copy(acts, a_own, local_sem.at[0]),
        pltpu.make_async_copy(gate, w_own.at[0], local_sem.at[1]),
        pltpu.make_async_copy(up, w_own.at[1], local_sem.at[2]),
        pltpu.make_async_copy(down, dn.at[pl.ds(0, width)], local_sem.at[3]),
    ]
    for c in loads:
        c.start()

    barrier = pltpu.get_barrier_semaphore()
    def greet(p):
        pl.semaphore_signal(barrier, inc=1, device_id=p, device_id_type=MESH)

    def choose(cond, one, two):
        return tuple(jnp.where(cond, a, b) for a, b in zip(one, two))

    for p in (choose(final, ahead_via, ahead), choose(first, behind_via, behind), twin, across):
        greet(p)

    @pl.when(jnp.logical_or(first, final))
    def _():
        greet(partner)
        greet(choose(final, ahead_other, behind_other))
        pl.semaphore_wait(barrier, 6)

    @pl.when(jnp.logical_not(jnp.logical_or(first, final)))
    def _():
        pl.semaphore_wait(barrier, 4)

    crossed = PASS + CROSS
    unit = feats * width // ND
    kw = unit // (2 * width)
    w1, w2, d1, d2, d3 = {}, {}, {}, {}, {}
    a1 = {}

    def send_w(at):
        def go():
            ds = pl.ds(at, kw)
            w1[at] = [
                Hop(s.at[ds], w_1.at[h, ds], v_w1.at[h, ds], ahead) for h, s in enumerate((gate, up))
            ]
            return w1[at]

        return kw * 2 * width / unit, go

    def relay_w(at):
        def go():
            for c in w1[at]:
                arrive(c)
            src = dst = pl.ds(at, kw)
            w2[at] = [
                Hop(w_1.at[h, src], w_2.at[h, dst], v_w2.at[h, dst], ahead) for h in range(2)
            ]
            return w2[at]

        return kw * 2 * width / unit, go

    def send_d(j):
        def go():
            at = pl.ds(j * (feats // ND), feats // ND)
            d1[j] = Hop(down.at[:, at], dn.at[pl.ds(width, width), at], v_d.at[0, :, at], ahead, mate=j % 2 == 0)
            return [d1[j]]

        return 1, go

    def relay_d(hop, j):
        def go():
            source, made = (d1, d2) if hop == 2 else (d2, d3)
            arrive(source[j])
            at = pl.ds(j * (feats // ND), feats // ND)
            made[j] = Hop(
                dn.at[pl.ds((hop - 1) * width, width), at],
                dn.at[pl.ds(hop * width, width), at],
                v_d.at[hop - 1, :, at],
                ahead,
                mate=j % 2 == 0,
            )
            return [made[j]]

        return 1, go

    def send_a(i):
        def go():
            ds = pl.ds(i * ra, ra)
            a1[i] = Hop(acts.at[ds], a_1.at[ds], v_a1.at[ds], behind)
            return [a1[i]]

        return ra * feats / unit, go

    ahead_stream = [send_w(at) for at in range(0, feats, kw)]
    ahead_stream += [relay_w(at) for at in range(0, feats, kw)]
    ahead_stream += [send_d(j) for j in range(ND)]
    ahead_stream += [relay_d(2, j) for j in range(ND)]
    ahead_stream += [relay_d(3, j) for j in range(ND)]
    back_stream = [send_a(i) for i in range(NA)]

    def weights(ref, at, kc):
        return [ref[0, pl.ds(at, kc), :], ref[1, pl.ds(at, kc), :]]

    def whole(a_ref, w_ref):
        kc = feats // 16
        acc[...] = jnp.zeros_like(acc)

        def step(k, _):
            at = pl.multiple_of(k * kc, kc)
            w = jnp.concatenate(weights(w_ref, at, kc), axis=1)
            acc[...] += dot(a_ref[:, pl.ds(at, kc)], w)
            return 0

        lax.fori_loop(0, feats // kc, step, 0)

    def reduce_1(buf, into):
        return remote(buf.at[1 - core], into, twin)

    def reduce_2(copy, buf, into, half):
        arrive(copy)
        into[...] = into[...] + buf[core]
        return remote(into.at[1 - y], half, across)

    def reduce_3(copy, into, half):
        arrive(copy)
        return into[y] + half[...]

    def gather_1(at):
        return remote(hid.at[at], hid.at[at], twin), remote(hid.at[at], hid.at[at], across)

    def gather_2(copies, at):
        arrive(copies[1])
        return copies[0], remote(hid.at[at], hid.at[at], twin)

    todo = {}

    def when(step):
        def note(f):
            todo.setdefault(step, []).append(f)
            return f

        return note

    arrivals = []
    state = {}

    def spot(s, block):
        at = pl.multiple_of(block * qr, qr)
        return pl.ds(at, qr), pl.ds(s * width, width)

    theirs = 2 * core + 1 - y

    def pair(s, step, a_ref, w_ref, ready, late=None):
        steps = [step, step + 1 if late is None else late]
        steps += [steps[-1] + LAG]
        if s > 1:
            steps += [steps[-1] + crossed]
        steps += [steps[-1] + LAG]
        steps = [min(at, last) for at in steps]

        if s > 1 and steps[2] + PASS - 1 < steps[3]:
            when(steps[2] + PASS - 1)(lambda: state[s].pass_on())

        @when(steps[0])
        def _():
            ready()
            whole(a_ref, w_ref)
            for q in range(4):
                part[s, q // 2, q % 2] = acc[q * qr : (q + 1) * qr, :]
            state[s] = reduce_1(part.at[s], part_in.at[s])

        @when(steps[1])
        def _():
            state[s] = reduce_2(state[s], part.at[s], part_in.at[s], half_in.at[s])

        @when(steps[2])
        def _():
            total = reduce_3(state[s], part_in.at[s], half_in.at[s])
            value = silu_times(total[:, :width], total[:, width:]).astype(BF16)
            if s > 1:
                fwd[s - 2] = value
                state[s] = Hop(
                    fwd.at[s - 2], hid.at[spot(s, mine)], v_fwd.at[s - 2], ahead, hid.at[spot(s, theirs)]
                )
            else:
                hid[spot(s, mine)] = value
                state[s] = gather_1(spot(s, mine))

        if s > 1:

            @when(steps[3])
            def _():
                state[s].pass_on()
                arrive(state[s])
                state[s] = gather_1(spot(s, mine))

        @when(steps[-1])
        def _():
            arrivals.extend(gather_2(state[s], spot(s, theirs)))

    def loaded():
        for c in loads:
            c.wait()

    def of_w(w):
        def ready():
            for cs in w.values():
                for c in cs:
                    arrive(c)
            for c in a1.values():
                if w is w2:
                    arrive(c)

        return ready

    def of_a():
        for c in a1.values():
            arrive(c)

    size_w, size_a = feats * 2 * width / unit, rows * feats / unit
    last = int(2 * size_w + 3 * ND) + 1
    quiet = int(size_a) + 1
    pair(0, 0, a_own, w_own, loaded, quiet)
    pair(1, int(size_w) - 1 + crossed, a_own, w_1, of_w(w1), quiet + 2)
    pair(2, int(size_a) - 1 + crossed, a_1, w_1, of_a)
    pair(3, int(max(size_a, 2 * size_w)) + crossed, a_1, w_2, of_w(w2))

    queues = []
    for stream in (ahead_stream, back_stream):
        due, total = [], 0.0
        for size, go in stream:
            due.append((int(total + 1e-6), go))
            total += size
        queues.append([due, 0, []])
    for step in range(last + 1):
        for queue in queues:
            due, place, sent = queue
            for copies in [c for at, c in sent if at == step - PASS]:
                for c in copies:
                    c.pass_on()
            for copies in [c for at, c in sent if at == step - WINDOW]:
                for c in copies:
                    c.wait_send()
            while place < len(due) and due[place][0] <= step:
                sent.append((step, due[place][1]()))
                place += 1
            queue[1] = place
        for f in todo.get(step, []):
            f()
            if step == last:
                for c in hops:
                    c.pass_on()
        if step == last:
            for c in hops:
                c.pass_on()
    for due, place, _ in queues:
        assert place == len(due)
    assert len(started) <= COPIES

    for c in arrivals:
        arrive(c)
    stores = []
    for e in range(ND):
        arrive(d3[e])
        cols = feats // ND
        at = pl.ds(e * cols, cols)
        o_buf[:, at] = dot(hid[...], dn[:, at]).astype(BF16)
        c = pltpu.make_async_copy(o_buf.at[:, at], out.at[:, at], local_sem.at[4 + e])
        c.start()
        stores.append(c)
    waited = {id(c) for _, _, sent in queues for at, cs in sent if at + WINDOW <= last for c in cs}
    for c in started:
        if id(c) not in waited:
            c.wait_send()
    for c in hops:
        pl.when(c.via)(c.second.wait_send)
    for c in stores:
        c.wait()


def body(n, acts, gate, up, down):
    rows, feats = acts.shape
    width = gate.shape[1]
    qr = rows // 4
    any_space = pl.BlockSpec(memory_space=pl.ANY)
    vmem = pltpu.VMEM
    return pl.pallas_call(
        functools.partial(kernel, n),
        out_shape=jax.ShapeDtypeStruct((rows, feats), BF16),
        in_specs=[any_space] * 4,
        out_specs=any_space,
        scratch_shapes=[
            vmem((rows, feats), BF16),
            vmem((rows, feats), BF16),
            vmem((2, feats, width), BF16),
            vmem((2, feats, width), BF16),
            vmem((2, feats, width), BF16),
            vmem((4 * width, feats), BF16),
            vmem((rows, 4 * width), BF16),
            vmem((rows, 2 * width), F32),
            vmem((4, 2, 2, qr, 2 * width), F32),
            vmem((4, 2, qr, 2 * width), F32),
            vmem((4, qr, 2 * width), F32),
            vmem((2, qr, width), BF16),
            vmem((rows, feats), BF16),
            vmem((2, feats, width), BF16),
            vmem((2, feats, width), BF16),
            vmem((3, width, feats), BF16),
            vmem((rows, feats), BF16),
            vmem((2, qr, width), BF16),
            pltpu.SemaphoreType.DMA((COPIES,)),
            pltpu.SemaphoreType.DMA((COPIES,)),
            pltpu.SemaphoreType.DMA((COPIES,)),
            pltpu.SemaphoreType.DMA((COPIES,)),
            pltpu.SemaphoreType.DMA((4 + ND,)),
        ],
        compiler_params=pltpu.CompilerParams(
            collective_id=0, has_side_effects=True, vmem_limit_bytes=56 * 2**20
        ),
    )(acts, gate, up, down)


def solution(mesh):
    n = mesh.shape["loop"]
    placed = (P("loop", "rep"), P("rep", "loop"), P("rep", "loop"), P("loop", "rep"))

    step = functools.partial(body, n)

    return jax.shard_map(
        step, mesh=mesh, in_specs=placed, out_specs=P("loop", "rep"), check_vma=False
    )
```

time: 240 us -> 195 us (0.81)
  Pallas kernels: 235 us -> 190 us
    pallas_call x1, Pallas kernels: 235 us -> 190 us  [body(): pl.pallas_call(functools.partial(kernel, n), out_shape=jax.ShapeDtypeStru...]
where the time goes in v3:
time: 195 us
  Pallas kernels  190 us (97%)
  local copies, waits for them, and re-layouts  4.7 us (2%)
    pallas_call x1, Pallas kernels, body(): pl.pallas_call(functools.partial(kernel, n), out_shape=jax.ShapeDtypeStru...  190 us
    unnamed x1, local copies, waits for them, and re-layouts  4.7 us

profile of v3, /device:TPU:1, one launch (start us, length us, event | category | flops | bytes accessed | tf_op | source)
XLA Modules:
  0.0 195.1 jit_solution(1982721573789101902)
XLA Ops:
  0.0 190.4 %shard_map.46 = bf16[512,4096]{1,0:T(8,128)(2,1)} custom-call(bf16[512,4096]{1,0:T(8,128)(2,1)} %acts.1, bf16[4096,128]{1,0:T(8,128)(2,1)} %gate.1, bf16[4096,128]{1,0:T(8,128)(2,1)} %up.1, bf16[128,4096]{1,0:T(8,128)(2,1)} %down.1), custom_call_target="tpu_custom_call" | custom-call | tf_op jit(solution)/shard_map/pallas_call | solution.py:442
  190.4 4.7 %copy.6 = bf16[512,4096]{1,0:T(8,128)(2,1)} copy(bf16[512,4096]{1,0:T(8,128)(2,1)} %shard_map.46) | data formatting | bytes 8388608

commit v4 on v3

--- a/solution.py
+++ b/solution.py
@@ -10,9 +10,9 @@
 MESH = pl.DeviceIdType.MESH
 NA = 16
 ND = 8
-WINDOW = 3
-PASS = 4
-CROSS = 3
+WINDOW = 4
+PASS = 3
+CROSS = 4
 LAG = 5
 COPIES = 136
 F32 = jnp.float32

time: 195 us -> 194 us (level)
  no operation moved by 1% of the time
where the time goes in v4:
time: 194 us; the launch traced here: 193 us
  Pallas kernels  189 us (97%)
  local copies, waits for them, and re-layouts  4.7 us (2%)
    pallas_call x1, Pallas kernels, body(): pl.pallas_call(functools.partial(kernel, n), out_shape=jax.ShapeDtypeStru...  189 us
    unnamed x1, local copies, waits for them, and re-layouts  4.7 us

profile of v4, /device:TPU:1, one launch (start us, length us, event | category | flops | bytes accessed | tf_op | source)
XLA Modules:
  0.0 193.5 jit_solution(16152844106087235427)
XLA Ops:
  0.0 188.8 %shard_map.46 = bf16[512,4096]{1,0:T(8,128)(2,1)} custom-call(bf16[512,4096]{1,0:T(8,128)(2,1)} %acts.1, bf16[4096,128]{1,0:T(8,128)(2,1)} %gate.1, bf16[4096,128]{1,0:T(8,128)(2,1)} %up.1, bf16[128,4096]{1,0:T(8,128)(2,1)} %down.1), custom_call_target="tpu_custom_call" | custom-call | tf_op jit(solution)/shard_map/pallas_call | solution.py:442
  188.8 4.7 %copy.6 = bf16[512,4096]{1,0:T(8,128)(2,1)} copy(bf16[512,4096]{1,0:T(8,128)(2,1)} %shard_map.46) | data formatting | bytes 8388608

commit v5 on v4

--- a/solution.py
+++ b/solution.py
@@ -10,6 +10,7 @@
 MESH = pl.DeviceIdType.MESH
 NA = 16
 ND = 8
+NE = 16
 WINDOW = 4
 PASS = 3
 CROSS = 4
@@ -222,11 +223,11 @@
 
         return 1, go
 
-    def relay_d(hop, j):
+    def relay_d(hop, j, count):
         def go():
             source, made = (d1, d2) if hop == 2 else (d2, d3)
-            arrive(source[j])
-            at = pl.ds(j * (feats // ND), feats // ND)
+            arrive(source[j * ND // count])
+            at = pl.ds(j * (feats // count), feats // count)
             made[j] = Hop(
                 dn.at[pl.ds((hop - 1) * width, width), at],
                 dn.at[pl.ds(hop * width, width), at],
@@ -236,7 +237,7 @@
             )
             return [made[j]]
 
-        return 1, go
+        return ND / count, go
 
     def send_a(i):
         def go():
@@ -249,8 +250,8 @@
     ahead_stream = [send_w(at) for at in range(0, feats, kw)]
     ahead_stream += [relay_w(at) for at in range(0, feats, kw)]
     ahead_stream += [send_d(j) for j in range(ND)]
-    ahead_stream += [relay_d(2, j) for j in range(ND)]
-    ahead_stream += [relay_d(3, j) for j in range(ND)]
+    ahead_stream += [relay_d(2, j, ND) for j in range(ND)]
+    ahead_stream += [relay_d(3, j, NE) for j in range(NE)]
     back_stream = [send_a(i) for i in range(NA)]
 
     def weights(ref, at, kc):
@@ -415,9 +416,9 @@
     for c in arrivals:
         arrive(c)
     stores = []
-    for e in range(ND):
+    for e in range(NE):
         arrive(d3[e])
-        cols = feats // ND
+        cols = feats // NE
         at = pl.ds(e * cols, cols)
         o_buf[:, at] = dot(hid[...], dn[:, at]).astype(BF16)
         c = pltpu.make_async_copy(o_buf.at[:, at], out.at[:, at], local_sem.at[4 + e])
@@ -467,7 +468,7 @@
             pltpu.SemaphoreType.DMA((COPIES,)),
             pltpu.SemaphoreType.DMA((COPIES,)),
             pltpu.SemaphoreType.DMA((COPIES,)),
-            pltpu.SemaphoreType.DMA((4 + ND,)),
+            pltpu.SemaphoreType.DMA((4 + NE,)),
         ],
         compiler_params=pltpu.CompilerParams(
             collective_id=0, has_side_effects=True, vmem_limit_bytes=56 * 2**20

time: 194 us -> 194 us (level)
  no operation moved by 1% of the time
where the time goes in v5:
time: 194 us
  Pallas kernels  189 us (97%)
  local copies, waits for them, and re-layouts  4.7 us (2%)
    pallas_call x1, Pallas kernels, body(): pl.pallas_call(functools.partial(kernel, n), out_shape=jax.ShapeDtypeStru...  189 us
    unnamed x1, local copies, waits for them, and re-layouts  4.7 us

profile of v5, /device:TPU:1, one launch (start us, length us, event | category | flops | bytes accessed | tf_op | source)
XLA Modules:
  0.0 193.6 jit_solution(17403409162562297352)
XLA Ops:
  0.0 188.9 %shard_map.46 = bf16[512,4096]{1,0:T(8,128)(2,1)} custom-call(bf16[512,4096]{1,0:T(8,128)(2,1)} %acts.1, bf16[4096,128]{1,0:T(8,128)(2,1)} %gate.1, bf16[4096,128]{1,0:T(8,128)(2,1)} %up.1, bf16[128,4096]{1,0:T(8,128)(2,1)} %down.1), custom_call_target="tpu_custom_call" | custom-call | tf_op jit(solution)/shard_map/pallas_call | solution.py:443
  188.9 4.7 %copy.6 = bf16[512,4096]{1,0:T(8,128)(2,1)} copy(bf16[512,4096]{1,0:T(8,128)(2,1)} %shard_map.46) | data formatting | bytes 8388608
